TPU v7x, 128 devices: a whole 4x4x4 slice. The times are simulated.
128 devices in a mesh: grp: 4 (over x), fsdp: 32 (over y, z, core).
Axes of the slice: x: 4, y: 4, z: 4, core: 2. Of those that a mesh axis runs over, the one named last changes fastest.
Arguments:
- tokens: bfloat16 [8192, 4096], P('fsdp'), may hold values from -550 to 550
- attn_gain: float32 [4096], replicated, may hold values from 0.1 to 1.9
- ffn_gain: float32 [4096], replicated, may hold values from 0.1 to 1.9
- w_query: bfloat16 [4096, 4096], P('fsdp', 'grp'), may hold values from -2.421875 to 2.421875
- w_key: bfloat16 [4096, 256], P('fsdp'), may hold values from -0.078125 to 0.078125
- value_weight: bfloat16 [4096, 256], P('fsdp'), may hold values from -0.09375 to 0.09375
- w_out: bfloat16 [4096, 4096], P('grp', 'fsdp'), may hold values from -0.5 to 0.5
- routes: int32 [8192, 8], P('fsdp'), may hold values from 0 to 127, all different within a row; in each aligned block of 256 rows (0 to 255, 256 to 511, ...) at most 24 rows name the same one
- route_probs: bfloat16 [8192, 8], P('fsdp'), may hold values from 0.049804688 to 0.3984375
- w_gate_up: bfloat16 [128, 4096, 1536], P(('grp', 'fsdp')), may hold values from -0.09375 to 0.09375
- w_down: bfloat16 [128, 768, 4096], P(('grp', 'fsdp')), may hold values from -0.21875 to 0.21875
Outputs:
- attn_branch: bfloat16 [8192, 4096], P('fsdp')
- layer_out: bfloat16 [8192, 4096], P('fsdp', 'grp')
Inputs may be any that keep to these rules, and one draw needn't show every extreme that they name: `routes`: each row names 8 different experts. Among the 256 rows of one device (aligned blocks), no expert is named more than 24 times, a bound that some block reaches.
All inputs are finite; a program needn't handle non-finite values.
Results may differ from a plain program's by a relative error of at most 0.015.
Values may be sent and summed in bfloat16 or wider, within the bound.
No kernel may reach another device: no remote copies, remote signals or barrier semaphores. Data moves between devices by JAX's collectives and lax.ppermute only.
A program may use at most 128 MiB of HBM per device.

v0:
```python
import jax
import jax.numpy as jnp
from jax import lax
from jax.sharding import PartitionSpec as P

KEY_VALUE_HEADS = 2
HEAD_DIMENSION = 128
FFW = 768
EPSILON = 1e-06
FLOOR_SCORE = -1e30


def rms_scale(row_data, gain):
    floats = row_data.astype(jnp.float32)
    mean_sq = jnp.mean(floats * floats, axis=-1, keepdims=True)
    return (floats * lax.rsqrt(mean_sq + EPSILON) * gain).astype(jnp.bfloat16)


def attend_block(state, query_bf, key_block, value_block, key_start, positions):
    row_best, row_total, weighted = state
    scores = jnp.einsum(
        "thd,kd->thk", query_bf, key_block, preferred_element_type=jnp.float32
    ) * HEAD_DIMENSION ** (-0.5)
    key_pos = key_start + jnp.arange(key_block.shape[0], dtype=jnp.int32)
    allowed = (key_pos[None, :] <= positions[:, None])[:, None, :]
    masked = jnp.where(allowed, scores, FLOOR_SCORE)
    new_best = jnp.maximum(row_best, jnp.max(masked, axis=2))
    weights = jnp.where(allowed, jnp.exp(masked - new_best[:, :, None]), 0.0)
    rescale = jnp.exp(row_best - new_best)
    row_total = row_total * rescale + jnp.sum(weights, axis=2)
    weighted = weighted * rescale[:, :, None] + jnp.einsum(
        "thk,kd->thd", weights.astype(jnp.bfloat16), value_block, preferred_element_type=jnp.float32
    )
    return (new_best, row_total, weighted)


def on_device(
    tokens,
    attn_gain,
    ffn_gain,
    w_query,
    w_key,
    value_weight,
    w_out,
    routes,
    route_probs,
    w_gate_up,
    w_down,
):
    head_groups = lax.axis_size("grp")
    fsdp_size = lax.axis_size("fsdp")
    current_group = lax.axis_index("grp")
    my_rank = lax.axis_index("fsdp")
    tok_rows = tokens.shape[0]
    model_width = tokens.shape[1]
    head_width = w_query.shape[1]
    group_heads = head_width // HEAD_DIMENSION
    key_value_head = current_group * KEY_VALUE_HEADS // head_groups
    normed = rms_scale(tokens, attn_gain)
    key_cols = lax.dynamic_slice_in_dim(w_key, key_value_head * HEAD_DIMENSION, HEAD_DIMENSION, 1)
    value_cols = lax.dynamic_slice_in_dim(
        value_weight, key_value_head * HEAD_DIMENSION, HEAD_DIMENSION, 1
    )
    query = jnp.dot(
        normed,
        lax.all_gather(w_query, "fsdp", axis=0, tiled=True),
        preferred_element_type=jnp.float32,
    )
    key_local = jnp.dot(
        normed,
        lax.all_gather(key_cols, "fsdp", axis=0, tiled=True),
        preferred_element_type=jnp.float32,
    )
    value_local = jnp.dot(
        normed,
        lax.all_gather(value_cols, "fsdp", axis=0, tiled=True),
        preferred_element_type=jnp.float32,
    )
    query_bf = query.astype(jnp.bfloat16).reshape(tok_rows, group_heads, HEAD_DIMENSION)
    key_local = key_local.astype(jnp.bfloat16)
    value_local = value_local.astype(jnp.bfloat16)
    first_row = my_rank * tok_rows
    positions = first_row + jnp.arange(tok_rows, dtype=jnp.int32)
    last_query = first_row + tok_rows - 1
    attend_init = (
        jnp.full((tok_rows, group_heads), FLOOR_SCORE, jnp.float32),
        jnp.zeros((tok_rows, group_heads), jnp.float32),
        jnp.zeros((tok_rows, group_heads, HEAD_DIMENSION), jnp.float32),
    )
    state = attend_init
    key_rows = lax.all_gather(key_local, "fsdp", axis=0, tiled=True)
    value_rows = lax.all_gather(value_local, "fsdp", axis=0, tiled=True)
    row_count = key_rows.shape[0]
    key_span = 1024

    def visit(running, step_index):
        block_start = step_index * key_span
        key_block = lax.dynamic_slice_in_dim(key_rows, block_start, key_span, 0)
        value_block = lax.dynamic_slice_in_dim(value_rows, block_start, key_span, 0)
        needed = block_start <= last_query
        running = lax.cond(
            needed,
            lambda inner: attend_block(
                inner, query_bf, key_block, value_block, block_start, positions
            ),
            lambda inner: inner,
            running,
        )
        return (running, None)

    state, _ = lax.scan(visit, state, jnp.arange(row_count // key_span, dtype=jnp.int32))
    row_best, row_total, weighted = state
    attended = (weighted / row_total[:, :, None]).astype(jnp.bfloat16).reshape(tok_rows, head_width)
    head_part = jnp.dot(
        attended,
        lax.all_gather(w_out, "fsdp", axis=1, tiled=True),
        preferred_element_type=jnp.float32,
    ).astype(jnp.bfloat16)
    attn_branch = lax.psum(head_part.astype(jnp.float32).astype(jnp.bfloat16), "grp")
    resid = (tokens.astype(jnp.float32) + attn_branch.astype(jnp.float32)).astype(jnp.bfloat16)
    ffn_in = rms_scale(resid, ffn_gain)
    top_count = routes.shape[1]
    experts_all = head_groups * fsdp_size
    capacity = max(2, 3 * tok_rows * top_count // (2 * experts_all))
    group_rows = fsdp_size * capacity
    flat_routes = routes.reshape(-1)
    expert_hits = (
        flat_routes[:, None] == jnp.arange(experts_all, dtype=jnp.int32)[None, :]
    ).astype(jnp.int32)
    slot_ids = jnp.sum(jnp.cumsum(expert_hits, axis=0) * expert_hits, axis=1) - 1
    target = flat_routes * capacity + slot_ids
    local_target = target - current_group * group_rows
    slot_match = (
        local_target[:, None] == jnp.arange(group_rows, dtype=jnp.int32)[None, :]
    ).reshape(tok_rows, top_count, group_rows)
    chosen = jnp.any(slot_match, axis=1).astype(jnp.bfloat16)
    outbound = (
        jnp.einsum("tr,td->rd", chosen, ffn_in, preferred_element_type=jnp.float32)
        .astype(jnp.bfloat16)
        .reshape(fsdp_size, capacity, model_width)
    )
    gate_proj = w_gate_up[0]
    down_proj = w_down[0]
    col_width = model_width // head_groups
    arrived = lax.all_to_all(outbound, "fsdp", split_axis=0, concat_axis=0, tiled=True)
    slot_count = arrived.shape[1]
    arrived_rows = arrived.reshape(-1, model_width)
    gate_up = jnp.dot(arrived_rows, gate_proj, preferred_element_type=jnp.float32)
    hidden = (jax.nn.silu(gate_up[:, :FFW]) * gate_up[:, FFW:]).astype(jnp.bfloat16)
    result = jnp.dot(hidden, down_proj, preferred_element_type=jnp.float32).astype(jnp.bfloat16)
    returned = lax.all_to_all(
        result.reshape(fsdp_size, slot_count, model_width),
        "fsdp",
        split_axis=0,
        concat_axis=0,
        tiled=True,
    )
    mixing = jnp.sum(jnp.where(slot_match, route_probs[:, :, None], 0.0), axis=1)
    group_part = jnp.dot(
        mixing, returned.reshape(group_rows, model_width), preferred_element_type=jnp.float32
    ).astype(jnp.bfloat16)
    expert_mix = lax.psum_scatter(
        group_part.astype(jnp.float32).astype(jnp.bfloat16), "grp", scatter_dimension=1, tiled=True
    ).astype(jnp.float32)
    own_cols = lax.dynamic_slice_in_dim(resid, current_group * col_width, col_width, 1)
    layer_out = (own_cols.astype(jnp.float32) + expert_mix).astype(jnp.bfloat16)
    return (attn_branch, layer_out)


def solution(mesh):
    placed = (
        P("fsdp", None),
        P(),
        P(),
        P("fsdp", "grp"),
        P("fsdp", None),
        P("fsdp", None),
        P("grp", "fsdp"),
        P("fsdp", None),
        P("fsdp", None),
        P(("grp", "fsdp"), None, None),
        P(("grp", "fsdp"), None, None),
    )
    return jax.shard_map(
        on_device,
        mesh=mesh,
        in_specs=placed,
        out_specs=(P("fsdp", None), P("fsdp", "grp")),
        check_vma=False,
    )
```

profile of v0, /device:TPU:1, one launch (start us, length us, event | category | flops | bytes accessed | tf_op | source)
XLA Modules:
  0.0 637.4 jit_solution(16513742144885637357)
XLA Ops:
  13.0 44.5 %all-gather.13.cloned.1.call-done = bf16[4096,128]{1,0:T(8,128)(2,1)} async-done(((bf16[128,128]{1,0:T(8,128)(2,1)}), bf16[4096,128]{1,0:T(8,128)(2,1)}) %all-gather.13.cloned.1.call-update) | async-done | bytes 1048592 | tf_op jit(solution)/shard_map/all_gather | solution.py:76
  57.5 3.3 convolution_convert_fusion.5
  60.9 41.6 %all-gather.7.cloned.1.call-done = bf16[4096,128]{1,0:T(8,128)(2,1)} async-done(((bf16[128,128]{1,0:T(8,128)(2,1)}), bf16[4096,128]{1,0:T(8,128)(2,1)}) %all-gather.7.cloned.1.call-update) | async-done | bytes 1048592 | tf_op jit(solution)/shard_map/all_gather | solution.py:71
  102.4 2.7 convolution_convert_fusion.6
  105.8 51.2 %all-gather.11.cloned.1.call-done = bf16[4096,1024]{1,0:T(8,128)(2,1)} async-done(((bf16[128,1024]{1,0:T(8,128)(2,1)}), bf16[4096,1024]{1,0:T(8,128)(2,1)}) %all-gather.11.cloned.1.call-update) | async-done | bytes 8388624 | tf_op jit(solution)/shard_map/all_gather | solution.py:66
  157.0 5.7 fusion.38
  162.8 40.4 %all-gather.15.cloned.1.call-done = bf16[8192,128]{1,0:T(8,128)(2,1)} async-done(((bf16[256,128]{1,0:T(8,128)(2,1)}), bf16[8192,128]{1,0:T(8,128)(2,1)}) %all-gather.15.cloned.1.call-update) | async-done | bytes 2097168 | tf_op jit(solution)/shard_map/all_gather | solution.py:92
  203.2 45.9 %all-gather.9.cloned.1.call-done = bf16[8192,128]{1,0:T(8,128)(2,1)} async-done(((bf16[256,128]{1,0:T(8,128)(2,1)}), bf16[8192,128]{1,0:T(8,128)(2,1)}) %all-gather.9.cloned.1.call-update) | async-done | bytes 2097168 | tf_op jit(solution)/shard_map/all_gather | solution.py:91
  249.2 19.2 %while.15 = (s32[]{:T(128)}, f32[256,8]{0,1:T(8,128)S(1)}, f32[256,8]{0,1:T(8,128)S(1)}, f32[256,8,128]{2,0,1:T(8,128)S(1)}, s32[8]{0:T(128)S(1)}, /*index=5*/s3...) while((s32[]{:T(128)}, f32[256,8]{0,1:T(8,128)S(1)}, ...), condition=%wide.region_6.7_spmd.clone, body=%wide.region_1.6_spmd.clone.sunk | while | flops 1101796608 | bytes 29503820 | solution.py:111
  250.7 8.7 %conditional.3 = ((f32[256,8]{0,1:T(8,128)S(1)}, f32[256,8]{0,1:T(8,128)S(1)}, f32[256,8,128]{2,0,1:T(8,128)S(1)})) conditional(s32[]{:T(128)} %convert_element_type.154, (f32[256,8]{0,1:T(8,128)S(1)}, f32[256,8]{0,1:T(8,128)S(1)}, f32[256,8,128]{2,0,1:T(8,128)S(1)}) %tuple.52, (s32[]{:T(128)}, s32[]{:T(128)}, bf16[8192,128]{1,0:T(8,128)(2,1)}, ...), branch_computations={%region_2.2_spmd, %region_3.5_spmd} | conditional | flops 1101796608 | bytes 29502546 | solution.py:101
  250.9 2.4 fusion.2
  255.4 3.9 fusion.8
  268.9 41.3 %all-gather.17.cloned.1.call-done = bf16[1024,4096]{1,0:T(8,128)(2,1)} async-done(((bf16[1024,128]{1,0:T(8,128)(2,1)}), bf16[1024,4096]{1,0:T(8,128)(2,1)}) %all-gather.17.cloned.1.call-update) | async-done | bytes 8388624 | tf_op jit(solution)/shard_map/all_gather | solution.py:116
  310.1 7.1 %convolution_convert_fusion.2 = bf16[256,4096]{1,0:T(8,128)(2,1)} fusion(bf16[256,1024]{0,1:T(8,128)(2,1)S(1)} %bitcast.62, bf16[1024,4096]{1,0:T(8,128)(2,1)} %all-gather.17.cloned.1.call-done), kind=kOutput, calls=%fused_computation.37 | convolution fusion | flops 2148532224 | bytes 11010048 | tf_op jit(solution)/shard_map/dot_general | solution.py:114
  321.8 72.3 %all-reduce.2.cloned.1.call-done = bf16[256,4096]{1,0:T(8,128)(2,1)} async-done(((bf16[256,4096]{1,0:T(8,128)(2,1)}), bf16[256,4096]{1,0:T(8,128)(2,1)}) %all-reduce.2.cloned.1.call-update) | async-done | bytes 2097168 | tf_op jit(solution)/shard_map/psum | solution.py:119
  394.1 3.2 fusion.26
  399.3 80.9 %all_to_all.10 = bf16[32,24,4096]{2,1,0:T(8,128)(2,1)S(1)} all-to-all(bf16[32,24,4096]{2,1,0:T(8,128)(2,1)S(1)} %bitcast.58), channel_id=1, replica_groups=mesh['grp'=4,'fsdp'=32] {'fsdp'}, dimensions={0} | all-to-all | bytes 12582912 | tf_op jit(solution)/shard_map/all_to_all | solution.py:145
  480.2 11.7 %fusion.21 = f32[768,1536]{1,0:T(8,128)} fusion(bf16[768,4096]{1,0:T(8,128)(2,1)S(1)} %bitcast.61, bf16[1,4096,1536]{2,1,0:T(8,128)(2,1)S(1)} %bitcast.64), kind=kOutput, calls=%fused_computation.24 | convolution fusion | flops 9663676416 | bytes 23592960 | tf_op jit(solution)/shard_map/dot_general | solution.py:148
  491.9 10.3 %convolution_convert_fusion.1 = bf16[768,4096]{1,0:T(8,128)(2,1)} fusion(bf16[1,768,4096]{2,1,0:T(8,128)(2,1)} %param.25, f32[768,1536]{1,0:T(8,128)} %fusion.21), kind=kOutput, calls=%fused_computation.27 | convolution fusion | flops 4838522880 | bytes 17301504 | tf_op jit(solution)/shard_map/dot_general | solution.py:150
  502.2 4.8 all-to-all-start.1
  509.6 75.3 %all-to-all-done.1 = bf16[32,24,4096]{2,1,0:T(8,128)(2,1)} async-done(((bf16[32,24,4096]{2,1,0:T(8,128)(2,1)}), bf16[32,24,4096]{2,1,0:T(8,128)(2,1)}, u32[]{:S(2)}, u32[]{:S(2)}) %all-to-all-start.1) | async-done | bytes 6291488 | tf_op jit(solution)/shard_map/all_to_all | solution.py:151
  584.8 5.9 convolution_convert_fusion.3
  590.8 34.6 %reduce-scatter.2.cloned.1.call-done = bf16[256,1024]{1,0:T(8,128)(2,1)} async-done(((bf16[256,4096]{1,0:T(8,128)(2,1)}), bf16[256,1024]{1,0:T(8,128)(2,1)}) %reduce-scatter.2.cloned.1.call-update) | async-done | bytes 524304 | tf_op jit(solution)/shard_map/reduce_scatter | solution.py:162
  627.4 3.1 copy.70
  (100 shorter events, 25.1 us)
Async XLA Ops:
  7.2 0.8 copy-start
  7.2 95.3 %copy-start.2 = (bf16[256,4096]{1,0:T(8,128)(2,1)S(1)}, bf16[256,4096]{1,0:T(8,128)(2,1)}, u32[]{:S(2)}) copy-start(bf16[256,4096]{1,0:T(8,128)(2,1)} %param.15) | copy-start | bytes 6291460
  7.2 95.3 %copy-start.6 = (f32[4096]{0:T(1024)S(1)}, f32[4096]{0:T(1024)}, u32[]{:S(2)}) copy-start(f32[4096]{0:T(1024)} %param.16) | copy-start | bytes 49156
  7.2 50.3 %all-gather.13.cloned.1.call-start = ((), (), s32[]{:S(2)}) async-start(), calls=%async_computation.6 | async-start | bytes 1081344 | tf_op jit(solution)/shard_map/all_gather | solution.py:76
  8.7 93.8 %all-gather.7.cloned.1.call-start = ((), (), s32[]{:S(2)}) async-start(), calls=%async_computation.3 | async-start | bytes 1081344 | tf_op jit(solution)/shard_map/all_gather | solution.py:71
  10.1 146.8 %all-gather.11.cloned.1.call-start = ((), (), s32[]{:S(2)}) async-start(), calls=%async_computation.5 | async-start | bytes 8650752 | tf_op jit(solution)/shard_map/all_gather | solution.py:66
  10.8 192.3 %all-gather.15.cloned.1.call-start = ((), (), s32[]{:S(2)}) async-start(), calls=%async_computation.7 | async-start | bytes 2162688 | tf_op jit(solution)/shard_map/all_gather | solution.py:92
  60.8 188.3 %all-gather.9.cloned.1.call-start = ((), (), s32[]{:S(2)}) async-start(), calls=%async_computation.4 | async-start | bytes 2162688 | tf_op jit(solution)/shard_map/all_gather | solution.py:91
  105.1 205.0 %all-gather.17.cloned.1.call-start = ((), (), s32[]{:S(2)}) async-start(), calls=%async_computation.8 | async-start | bytes 8650752 | tf_op jit(solution)/shard_map/all_gather | solution.py:116
  105.7 288.4 %all-reduce.2.cloned.1.call-start = ((), (), s32[]{:S(2)}) async-start(), calls=%async_computation.9 | async-start | bytes 4194304 | tf_op jit(solution)/shard_map/psum | solution.py:119
  310.1 7.1 %copy-start.3 = (s32[256,8]{0,1:T(8,128)S(1)}, s32[256,8]{0,1:T(8,128)}, u32[]{:S(2)}) copy-start(s32[256,8]{0,1:T(8,128)} %param.22) | copy-start | bytes 24580
  318.5 78.8 %copy-start.4 = (f32[4096]{0:T(1024)S(1)}, f32[4096]{0:T(1024)}, u32[]{:S(2)}) copy-start(f32[4096]{0:T(1024)} %param.17) | copy-start | bytes 49156
  397.3 82.9 %slice-start = ((s8[12582912]{0:T(1024)(128)(4,1)}), s8[4194304]{0:T(1024)(128)(4,1)S(1)}, s32[]{:S(2)}) async-start(s8[12582912]{0:T(1024)(128)(4,1)} %bitcast.63), calls=%async_computation.11 | async-start | bytes 8388608
  397.3 82.9 %slice-start.1 = ((s8[12582912]{0:T(1024)(128)(4,1)}), s8[4194304]{0:T(1024)(128)(4,1)S(1)}, s32[]{:S(2)}) async-start(s8[12582912]{0:T(1024)(128)(4,1)} %bitcast.63), calls=%async_computation.12 | async-start | bytes 8388608
  399.3 80.9 %slice-start.2 = ((s8[12582912]{0:T(1024)(128)(4,1)}), s8[4194304]{0:T(1024)(128)(4,1)S(1)}, s32[]{:S(2)}) async-start(s8[12582912]{0:T(1024)(128)(4,1)} %bitcast.63), calls=%async_computation.13 | async-start | bytes 8388608
  502.2 4.9 copy-start.5
  502.2 82.7 %all-to-all-start.1 = ((bf16[32,24,4096]{2,1,0:T(8,128)(2,1)}), bf16[32,24,4096]{2,1,0:T(8,128)(2,1)}, u32[]{:S(2)}, u32[]{:S(2)}) async-start(bf16[32,24,4096]{2,1,0:T(8,128)(2,1)} %bitcast.60), calls=%async_computation.1 | async-start | bytes 12582912 | tf_op jit(solution)/shard_map/all_to_all | solution.py:151
  507.0 118.4 %reduce-scatter.2.cloned.1.call-start = ((), (), s32[]{:S(2)}) async-start(), calls=%async_computation.10 | async-start | bytes 2621440 | tf_op jit(solution)/shard_map/reduce_scatter | solution.py:162
  584.8 45.7 %copy-start.1 = (bf16[128,256]{1,0:T(8,128)(2,1)S(1)}, bf16[128,256]{1,0:T(8,128)(2,1)}, u32[]{:S(2)}) copy-start(bf16[128,256]{1,0:T(8,128)(2,1)} %param.20) | copy-start | bytes 196612
Sparse Core Ops, SparseCore 0:
  10.9 46.5 all-gather.12
  60.3 42.0 all-gather.6
  104.7 52.1 all-gather.10
  159.6 43.4 all-gather.14
  205.9 43.2 all-gather.8
  251.2 58.9 all-gather.16
  317.4 76.7 all-reduce.1
  590.9 34.4 reduce-scatter.1
where the time goes:
time: 638 us; the launch traced here: 637 us
  waiting for transfers between devices  448 us (70%)
  blocking collectives  80.9 us (13%)
  matrix products  55 us (9%)
  other arithmetic  15.4 us (2%)
  between operations  14.4 us (2%)
  local copies, waits for them, and re-layouts  12.3 us (2%)
    all_to_all x1, blocking collectives, on_device(): lax.all_to_all(outbound, 'fsdp', split_axis=0, concat_axis=0, tiled=True)  80.9 us
    all_to_all x1, waiting for transfers between devices, on_device(): lax.all_to_all(result.reshape(fsdp_size, slot_count, model_width), 'fsdp'...  75.3 us
    psum x1, waiting for transfers between devices, on_device(): lax.psum(head_part.astype(jnp.float32).astype(jnp.bfloat16), 'grp')  72.3 us
    all_gather x1, waiting for transfers between devices, on_device(): lax.all_gather(w_query, 'fsdp', axis=0, tiled=True)  51.2 us
    all_gather x1, waiting for transfers between devices, on_device(): key_rows = lax.all_gather(key_local, 'fsdp', axis=0, tiled=True)  45.9 us
    all_gather x1, waiting for transfers between devices, on_device(): lax.all_gather(value_cols, 'fsdp', axis=0, tiled=True)  44.5 us
    all_gather x1, waiting for transfers between devices, on_device(): lax.all_gather(key_cols, 'fsdp', axis=0, tiled=True)  41.6 us
    all_gather x1, waiting for transfers between devices, on_device(): lax.all_gather(w_out, 'fsdp', axis=1, tiled=True)  41.3 us
  transfers between devices with their start and end apart: 9, of which 9 were waited for; matrix products, arithmetic and copies ran while one was open for 6% of the time, Pallas kernels for 0%

commit v1 on v0

--- a/solution.py
+++ b/solution.py
@@ -2,6 +2,7 @@
 import jax.numpy as jnp
 from jax import lax
 from jax.sharding import PartitionSpec as P
+from jax.lax import all_to_all, psum
 
 KEY_VALUE_HEADS = 2
 HEAD_DIMENSION = 128
@@ -111,10 +112,17 @@
     state, _ = lax.scan(visit, state, jnp.arange(row_count // key_span, dtype=jnp.int32))
     row_best, row_total, weighted = state
     attended = (weighted / row_total[:, :, None]).astype(jnp.bfloat16).reshape(tok_rows, head_width)
+    see_hubs_by_axis = lambda content, dev_axis: jnp.concatenate(
+        all_to_all(
+            jnp.stack(psum(1, axis_name=dev_axis) * [content], 0),
+            axis_name=dev_axis,
+            split_axis=0,
+            concat_axis=0,
+        ),
+        1,
+    )
     head_part = jnp.dot(
-        attended,
-        lax.all_gather(w_out, "fsdp", axis=1, tiled=True),
-        preferred_element_type=jnp.float32,
+        attended, see_hubs_by_axis(w_out, "fsdp"), preferred_element_type=jnp.float32
     ).astype(jnp.bfloat16)
     attn_branch = lax.psum(head_part.astype(jnp.float32).astype(jnp.bfloat16), "grp")
     resid = (tokens.astype(jnp.float32) + attn_branch.astype(jnp.float32)).astype(jnp.bfloat16)

time: 638 us -> 710 us (1.11)
  waiting for transfers between devices: 448 us -> 510 us
    all_gather x1, waiting for transfers between devices: 41.6 us -> 97.3 us  [on_device(): lax.all_gather(key_cols, 'fsdp', axis=0, tiled=True)]
    all_gather x1 -> x0, waiting for transfers between devices: 41.3 us -> none  [on_device(): lax.all_gather(w_out, 'fsdp', axis=1, tiled=True)]
    psum x1, waiting for transfers between devices: 72.3 us -> 113 us  [on_device(): lax.psum(head_part.astype(jnp.float32).astype(jnp.bfloat16), 'grp')]
  transfers between devices with their start and end apart: 9 -> 9, of which waited for: 9 -> 8; matrix products, arithmetic and copies ran while one was open for 6% -> 6% of each run, Pallas kernels for 0% -> 0%
where the time goes in v1:
time: 710 us; the launch traced here: 709 us
  waiting for transfers between devices  510 us (72%)
  blocking collectives  80.9 us (11%)
  matrix products  55.1 us (8%)
  local copies, waits for them, and re-layouts  16.8 us (2%)
  other arithmetic  15.4 us (2%)
  between operations  14.5 us (2%)
  starting transfers between devices  10.5 us (1%)
    psum x1, waiting for transfers between devices, on_device(): lax.psum(head_part.astype(jnp.float32).astype(jnp.bfloat16), 'grp')  113 us
    all_gather x1, waiting for transfers between devices, on_device(): lax.all_gather(key_cols, 'fsdp', axis=0, tiled=True)  97.3 us
    all_to_all x1, blocking collectives, on_device(): lax.all_to_all(outbound, 'fsdp', split_axis=0, concat_axis=0, tiled=True)  80.9 us
    all_to_all x1, waiting for transfers between devices, on_device(): lax.all_to_all(result.reshape(fsdp_size, slot_count, model_width), 'fsdp'...  75.3 us
    all_gather x1, waiting for transfers between devices, on_device(): lax.all_gather(w_query, 'fsdp', axis=0, tiled=True)  57.6 us
    all_gather x1, waiting for transfers between devices, on_device(): key_rows = lax.all_gather(key_local, 'fsdp', axis=0, tiled=True)  45.9 us
    all_gather x1, waiting for transfers between devices, on_device(): lax.all_gather(value_cols, 'fsdp', axis=0, tiled=True)  44.5 us
    all_gather x1, waiting for transfers between devices, on_device(): value_rows = lax.all_gather(value_local, 'fsdp', axis=0, tiled=True)  40.3 us
  transfers between devices with their start and end apart: 9, of which 8 were waited for; matrix products, arithmetic and copies ran while one was open for 6% of the time, Pallas kernels for 0%

profile of v1, /device:TPU:1, one launch (start us, length us, event | category | flops | bytes accessed | tf_op | source)
XLA Modules:
  0.0 708.6 jit_solution(4817414455475620107)
XLA Ops:
  13.0 44.5 %all-gather.12.cloned.1.call-done = bf16[4096,128]{1,0:T(8,128)(2,1)} async-done(((bf16[128,128]{1,0:T(8,128)(2,1)}), bf16[4096,128]{1,0:T(8,128)(2,1)}) %all-gather.12.cloned.1.call-update) | async-done | bytes 1048592 | tf_op jit(solution)/shard_map/all_gather | solution.py:77
  57.5 3.3 convolution_convert_fusion.5
  61.0 4.3 stack.2
  65.3 5.4 all-to-all-start
  70.7 97.3 %all-gather.6.cloned.1.call-done = bf16[4096,128]{1,0:T(8,128)(2,1)} async-done(((bf16[128,128]{1,0:T(8,128)(2,1)}), bf16[4096,128]{1,0:T(8,128)(2,1)}) %all-gather.6.cloned.1.call-update) | async-done | bytes 1048592 | tf_op jit(solution)/shard_map/all_gather | solution.py:72
  168.0 2.7 convolution_convert_fusion.6
  170.7 57.6 %all-gather.10.cloned.1.call-done = bf16[4096,1024]{1,0:T(8,128)(2,1)} async-done(((bf16[128,1024]{1,0:T(8,128)(2,1)}), bf16[4096,1024]{1,0:T(8,128)(2,1)}) %all-gather.10.cloned.1.call-update) | async-done | bytes 8388624 | tf_op jit(solution)/shard_map/all_gather | solution.py:67
  228.3 5.8 fusion.38
  234.1 40.3 %all-gather.14.cloned.1.call-done = bf16[8192,128]{1,0:T(8,128)(2,1)} async-done(((bf16[256,128]{1,0:T(8,128)(2,1)}), bf16[8192,128]{1,0:T(8,128)(2,1)}) %all-gather.14.cloned.1.call-update) | async-done | bytes 2097168 | tf_op jit(solution)/shard_map/all_gather | solution.py:93
  274.5 45.9 %all-gather.8.cloned.1.call-done = bf16[8192,128]{1,0:T(8,128)(2,1)} async-done(((bf16[256,128]{1,0:T(8,128)(2,1)}), bf16[8192,128]{1,0:T(8,128)(2,1)}) %all-gather.8.cloned.1.call-update) | async-done | bytes 2097168 | tf_op jit(solution)/shard_map/all_gather | solution.py:92
  320.5 19.2 %while.15 = (s32[]{:T(128)}, f32[256,8]{0,1:T(8,128)S(1)}, f32[256,8]{0,1:T(8,128)S(1)}, f32[256,8,128]{2,0,1:T(8,128)S(1)}, s32[8]{0:T(128)S(1)}, /*index=5*/s3...) while((s32[]{:T(128)}, f32[256,8]{0,1:T(8,128)S(1)}, ...), condition=%wide.region_6.7_spmd.clone, body=%wide.region_1.6_spmd.clone.sunk | while | flops 1101796608 | bytes 29503820 | solution.py:112
  322.0 8.7 %conditional.3 = ((f32[256,8]{0,1:T(8,128)S(1)}, f32[256,8]{0,1:T(8,128)S(1)}, f32[256,8,128]{2,0,1:T(8,128)S(1)})) conditional(s32[]{:T(128)} %convert_element_type.154, (f32[256,8]{0,1:T(8,128)S(1)}, f32[256,8]{0,1:T(8,128)S(1)}, f32[256,8,128]{2,0,1:T(8,128)S(1)}) %tuple.52, (s32[]{:T(128)}, s32[]{:T(128)}, bf16[8192,128]{1,0:T(8,128)(2,1)}, ...), branch_computations={%region_2.2_spmd, %region_3.5_spmd} | conditional | flops 1101796608 | bytes 29502546 | solution.py:102
  326.7 3.9 fusion.8
  340.2 7.1 %convolution_convert_fusion.2 = bf16[256,4096]{1,0:T(8,128)(2,1)} fusion(bf16[256,1024]{0,1:T(8,128)(2,1)S(1)} %bitcast.65, bf16[1024,4096]{0,1:T(8,128)(2,1)} %bitcast.5), kind=kOutput, calls=%fused_computation.37 | convolution fusion | flops 2148532224 | bytes 11010048 | tf_op jit(solution)/shard_map/dot_general | solution.py:124
  351.9 113.5 %all-reduce.2.cloned.1.call-done = bf16[256,4096]{1,0:T(8,128)(2,1)} async-done(((bf16[256,4096]{1,0:T(8,128)(2,1)}), bf16[256,4096]{1,0:T(8,128)(2,1)}) %all-reduce.2.cloned.1.call-update) | async-done | bytes 2097168 | tf_op jit(solution)/shard_map/psum | solution.py:127
  465.4 3.2 fusion.26
  470.6 80.9 %all_to_all.15 = bf16[32,24,4096]{2,1,0:T(8,128)(2,1)S(1)} all-to-all(bf16[32,24,4096]{2,1,0:T(8,128)(2,1)S(1)} %bitcast.61), channel_id=1, replica_groups=mesh['grp'=4,'fsdp'=32] {'fsdp'}, dimensions={0} | all-to-all | bytes 12582912 | tf_op jit(solution)/shard_map/all_to_all | solution.py:153
  551.4 11.7 %fusion.21 = f32[768,1536]{1,0:T(8,128)} fusion(bf16[768,4096]{1,0:T(8,128)(2,1)S(1)} %bitcast.64, bf16[1,4096,1536]{2,1,0:T(8,128)(2,1)S(1)} %bitcast.67), kind=kOutput, calls=%fused_computation.24 | convolution fusion | flops 9663676416 | bytes 23592960 | tf_op jit(solution)/shard_map/dot_general | solution.py:156
  563.1 10.3 %convolution_convert_fusion.1 = bf16[768,4096]{1,0:T(8,128)(2,1)} fusion(bf16[1,768,4096]{2,1,0:T(8,128)(2,1)} %param.25, f32[768,1536]{1,0:T(8,128)} %fusion.21), kind=kOutput, calls=%fused_computation.27 | convolution fusion | flops 4838522880 | bytes 17301504 | tf_op jit(solution)/shard_map/dot_general | solution.py:158
  573.4 4.8 all-to-all-start.2
  580.8 75.3 %all-to-all-done.2 = bf16[32,24,4096]{2,1,0:T(8,128)(2,1)} async-done(((bf16[32,24,4096]{2,1,0:T(8,128)(2,1)}), bf16[32,24,4096]{2,1,0:T(8,128)(2,1)}, u32[]{:S(2)}, u32[]{:S(2)}) %all-to-all-start.2) | async-done | bytes 6291488 | tf_op jit(solution)/shard_map/all_to_all | solution.py:159
  656.1 5.9 convolution_convert_fusion.3
  662.0 34.6 %reduce-scatter.2.cloned.1.call-done = bf16[256,1024]{1,0:T(8,128)(2,1)} async-done(((bf16[256,4096]{1,0:T(8,128)(2,1)}), bf16[256,1024]{1,0:T(8,128)(2,1)}) %reduce-scatter.2.cloned.1.call-update) | async-done | bytes 524304 | tf_op jit(solution)/shard_map/reduce_scatter | solution.py:170
  698.7 3.1 copy.73
  (103 shorter events, 27.1 us)
Async XLA Ops:
  7.2 0.8 copy-start
  7.2 53.6 %copy-start.3 = (bf16[1024,128]{1,0:T(8,128)(2,1)S(1)}, bf16[1024,128]{1,0:T(8,128)(2,1)}, u32[]{:S(2)}) copy-start(bf16[1024,128]{1,0:T(8,128)(2,1)} %param.21) | copy-start | bytes 786436
  7.2 50.3 %all-gather.12.cloned.1.call-start = ((), (), s32[]{:S(2)}) async-start(), calls=%async_computation.7 | async-start | bytes 1081344 | tf_op jit(solution)/shard_map/all_gather | solution.py:77
  8.7 159.3 %all-gather.6.cloned.1.call-start = ((), (), s32[]{:S(2)}) async-start(), calls=%async_computation.4 | async-start | bytes 1081344 | tf_op jit(solution)/shard_map/all_gather | solution.py:72
  10.1 218.2 %all-gather.10.cloned.1.call-start = ((), (), s32[]{:S(2)}) async-start(), calls=%async_computation.6 | async-start | bytes 8650752 | tf_op jit(solution)/shard_map/all_gather | solution.py:67
  10.8 263.6 %all-gather.14.cloned.1.call-start = ((), (), s32[]{:S(2)}) async-start(), calls=%async_computation.8 | async-start | bytes 2162688 | tf_op jit(solution)/shard_map/all_gather | solution.py:93
  65.3 102.7 %copy-start.2 = (bf16[256,4096]{1,0:T(8,128)(2,1)S(1)}, bf16[256,4096]{1,0:T(8,128)(2,1)}, u32[]{:S(2)}) copy-start(bf16[256,4096]{1,0:T(8,128)(2,1)} %param.15) | copy-start | bytes 6291460
  65.3 102.7 %copy-start.7 = (f32[4096]{0:T(1024)S(1)}, f32[4096]{0:T(1024)}, u32[]{:S(2)}) copy-start(f32[4096]{0:T(1024)} %param.16) | copy-start | bytes 49156
  65.3 274.9 %all-to-all-start = ((bf16[32,1024,128]{1,2,0:T(8,128)(2,1)}), bf16[32,1024,128]{1,2,0:T(8,128)(2,1)}, u32[]{:S(2)}, u32[]{:S(2)}) async-start(bf16[32,1024,128]{1,2,0:T(8,128)(2,1)} %stack.2), calls=%async_computation | async-start | bytes 16777216 | tf_op jit(solution)/shard_map/all_to_all | solution.py:116
  70.6 249.8 %all-gather.8.cloned.1.call-start = ((), (), s32[]{:S(2)}) async-start(), calls=%async_computation.5 | async-start | bytes 2162688 | tf_op jit(solution)/shard_map/all_gather | solution.py:92
  170.7 294.7 %all-reduce.2.cloned.1.call-start = ((), (), s32[]{:S(2)}) async-start(), calls=%async_computation.9 | async-start | bytes 4194304 | tf_op jit(solution)/shard_map/psum | solution.py:127
  340.2 7.1 %copy-start.4 = (s32[256,8]{0,1:T(8,128)S(1)}, s32[256,8]{0,1:T(8,128)}, u32[]{:S(2)}) copy-start(s32[256,8]{0,1:T(8,128)} %param.22) | copy-start | bytes 24580
  348.6 119.9 %copy-start.5 = (f32[4096]{0:T(1024)S(1)}, f32[4096]{0:T(1024)}, u32[]{:S(2)}) copy-start(f32[4096]{0:T(1024)} %param.17) | copy-start | bytes 49156
  468.6 82.9 %slice-start = ((s8[12582912]{0:T(1024)(128)(4,1)}), s8[4194304]{0:T(1024)(128)(4,1)S(1)}, s32[]{:S(2)}) async-start(s8[12582912]{0:T(1024)(128)(4,1)} %bitcast.66), calls=%async_computation.11 | async-start | bytes 8388608
  468.6 82.9 %slice-start.1 = ((s8[12582912]{0:T(1024)(128)(4,1)}), s8[4194304]{0:T(1024)(128)(4,1)S(1)}, s32[]{:S(2)}) async-start(s8[12582912]{0:T(1024)(128)(4,1)} %bitcast.66), calls=%async_computation.12 | async-start | bytes 8388608
  470.5 80.9 %slice-start.2 = ((s8[12582912]{0:T(1024)(128)(4,1)}), s8[4194304]{0:T(1024)(128)(4,1)S(1)}, s32[]{:S(2)}) async-start(s8[12582912]{0:T(1024)(128)(4,1)} %bitcast.66), calls=%async_computation.13 | async-start | bytes 8388608
  573.4 4.9 copy-start.6
  573.4 82.7 %all-to-all-start.2 = ((bf16[32,24,4096]{2,1,0:T(8,128)(2,1)}), bf16[32,24,4096]{2,1,0:T(8,128)(2,1)}, u32[]{:S(2)}, u32[]{:S(2)}) async-start(bf16[32,24,4096]{2,1,0:T(8,128)(2,1)} %bitcast.63), calls=%async_computation.2 | async-start | bytes 12582912 | tf_op jit(solution)/shard_map/all_to_all | solution.py:159
  578.2 118.4 %reduce-scatter.2.cloned.1.call-start = ((), (), s32[]{:S(2)}) async-start(), calls=%async_computation.10 | async-start | bytes 2621440 | tf_op jit(solution)/shard_map/reduce_scatter | solution.py:170
  656.1 45.7 %copy-start.1 = (bf16[128,256]{1,0:T(8,128)(2,1)S(1)}, bf16[128,256]{1,0:T(8,128)(2,1)}, u32[]{:S(2)}) copy-start(bf16[128,256]{1,0:T(8,128)(2,1)} %param.20) | copy-start | bytes 196612
Sparse Core Ops, SparseCore 0:
  10.9 46.5 all-gather.11
  60.3 107.6 all-gather.5
  170.2 58.0 all-gather.9
  231.0 43.4 all-gather.13
  277.2 43.2 all-gather.7
  347.4 117.8 all-reduce.1
  662.2 34.4 reduce-scatter.1
